TPU v7x, 32 devices: a whole 2x2x4 slice. The times are simulated.
32 devices in a mesh: tm: 8 (over z, core), space: 4 (over y, x).
Axes of the slice: x: 2, y: 2, z: 4, core: 2. Of those that a mesh axis runs over, the one named last changes fastest.
Arguments:
- increment: float32 [8, 4, 137, 512], P('tm', None, None, 'space'), may hold values from -26 to 26
- courant: float32 [8, 4, 137, 512], P('tm', None, None, 'space'), may hold values from -0.9 to 0.9
- error_weight: float32 [4, 137], replicated, may hold values from 0.5 to 2
- obs_code: int32 [8, 4, 4, 128], P('tm', 'space'), may hold values from 0 to 280574, as said below
- obs_values: float32 [8, 4, 4, 3, 128], P('tm', 'space'), as said below
- obs_count: int32 [8, 4, 4], P('tm', 'space'), may hold values from 25 to 128, as said below
Outputs:
- new_increment: float32 [8, 4, 137, 512], P('tm', None, None, 'space')
- departures: float32 [8, 4, 4, 128], P('tm', 'space')
Inputs may be any that keep to these rules, and one draw needn't show every extreme that they name: `obs_code`: code = ((t * 4 + f) * 137 + l) * 128 + c for an observation of the state after step t + 1 of its sub-window, field f, level l, between columns c and c + 1 of the destination tile, c < 127; slots at or beyond the count carry no observation. `obs_values`: row 1 lies in [0, 1], row 2 in [0.5, 4]. `obs_count`: in every sub-window some destination tile receives 128 observations from every source tile.
All inputs are finite; a program needn't handle non-finite values.
Results may differ from a plain program's by a relative error of at most 0.0003.
Values sent between devices are 32-bit elements; how exact they have to be, the bound alone decides.
A program may use at most 64 MiB of HBM per device.

v0:
```python
import jax
import jax.numpy as jnp
from jax import lax
from jax.sharding import PartitionSpec as P


def padded_2(array, sides, width):
    for axis, dim in sides:
        size, length = (lax.axis_size(axis), array.shape[dim])
        up = [(i, (i + 1) % size) for i in range(size)]
        down = [(j, i) for i, j in up]
        last = lax.slice_in_dim(array, length - width, length, axis=dim)
        initial = lax.slice_in_dim(array, 0, width, axis=dim)
        before = lax.ppermute(last, axis, up)
        after = lax.ppermute(initial, axis, down)
        array = jnp.concatenate([before, array, after], axis=dim)
    return array


def passed_along(array, axis, by):
    size = lax.axis_size(axis)
    pairs = [(i, i + by) for i in range(size) if 0 <= i + by < size]
    return lax.ppermute(array, axis, pairs)


def on_device(increment, courant, error_weight, obs_code, obs_values, obs_count):
    start = increment[0]
    cour = courant[0]
    steps = cour.shape[0]
    per_state = start.size
    slots = obs_code.shape[-1]
    qinv = error_weight[:, :, None]
    code_in, values_in, count_in = (
        lax.all_to_all(obs_code, "space", split_axis=2, concat_axis=2, tiled=True),
        lax.all_to_all(obs_values, "space", split_axis=2, concat_axis=2, tiled=True),
        lax.all_to_all(obs_count, "space", split_axis=2, concat_axis=2, tiled=True),
    )
    code_in = code_in[0, 0]
    values_in = values_in[0, 0]
    flat = code_in % per_state
    when = code_in // per_state
    valid = jnp.arange(slots, dtype=jnp.int32)[None, :] < count_in[0, 0][:, None]
    innovation = values_in[:, 0, :]
    weight = values_in[:, 1, :]
    rinv = values_in[:, 2, :]
    margin = 1
    cour_pad = padded_2(cour, (("space", 2),), margin)
    left_pad = 0.5 * cour_pad * (1.0 + cour_pad)
    right_pad = 0.5 * cour_pad * (cour_pad - 1.0)
    centre = 1.0 - cour * cour
    seen_all = jnp.zeros(flat.shape, jnp.float32)
    left = left_pad[:, :, 1:-1]
    right = right_pad[:, :, 1:-1]
    state = start
    for step in range(steps):
        padded = padded_2(state, (("space", 2),), 1)
        state = (
            centre[step] * state + left[step] * padded[:, :, :-2] + right[step] * padded[:, :, 2:]
        )
        line = state.reshape(-1)
        seen = weight * line[flat] + (1.0 - weight) * line[flat + 1]
        seen_all = jnp.where(when == step, seen, seen_all)
    departed = jnp.where(valid, seen_all - innovation, 0.0)
    pushed = rinv * departed
    previous = passed_along(state, "tm", 1)
    jump_own = start - previous
    weighted_own = qinv * jump_own
    weighted_next = passed_along(weighted_own, "tm", -1)
    jump_part = jnp.sum(weighted_own * jump_own)
    target = when * per_state + flat
    forcing = jnp.zeros((steps * per_state,), jnp.float32)
    forcing = forcing.at[target].add(weight * pushed).at[target + 1].add((1.0 - weight) * pushed)
    forcing = forcing.reshape((steps,) + start.shape)
    lam = -weighted_next + forcing[steps - 1]
    for step in reversed(range(steps)):
        retreat_padded = padded_2(lam, (("space", 2),), 1)
        lam = (
            centre[step] * lam
            + left_pad[step][:, 2:] * retreat_padded[:, :, 2:]
            + right_pad[step][:, :-2] * retreat_padded[:, :, :-2]
        )
        if step > 0:
            lam = lam + forcing[step - 1]
    gradient = weighted_own + lam
    cost_part = 0.5 * (jump_part + jnp.sum(pushed * departed))
    norm_part = jnp.sum(gradient * gradient)
    cost, norm = lax.psum((cost_part, norm_part), ("tm", "space"))
    renewed = increment - cost / norm * gradient[None]
    returned = lax.all_to_all(
        departed[None, None], "space", split_axis=2, concat_axis=2, tiled=True
    )
    return (renewed, returned)


def solution(mesh):
    in_specs = (
        P("tm", None, None, "space"),
        P("tm", None, None, "space"),
        P(),
        P("tm", "space", None, None),
        P("tm", "space", None, None, None),
        P("tm", "space", None),
    )
    out_specs = (P("tm", None, None, "space"), P("tm", "space", None, None))
    return jax.shard_map(
        on_device, mesh=mesh, in_specs=in_specs, out_specs=out_specs, check_vma=False
    )
```

profile of v0, /device:TPU:0, one launch (start us, length us, event | category | flops | bytes accessed | tf_op | source)
XLA Modules:
  0.0 220.6 jit_solution(10533462246855914328)
XLA Ops:
  0.6 1.3 copy.83
  1.9 5.2 %all-to-all-start.1 = ((s32[1,1,4]{1,0,2:T(1,128)}), s32[1,1,4]{1,0,2:T(1,128)S(1)}, u32[]{:S(2)}, u32[]{:S(2)}) async-start(s32[1,1,4]{1,0,2:T(1,128)} %copy.83), calls=%async_computation.1 | async-start | bytes 4096 | tf_op jit(solution)/shard_map/all_to_all | solution.py:36
  7.1 1.2 copy.68
  8.3 2.1 collective-permute-start
  13.2 1.1 collective-permute-start.2
  14.3 1.9 collective-permute-start.3
  16.2 3.2 %all-to-all-start.2 = ((s32[1,1,4,128]{3,1,0,2:T(1,128)}), s32[1,1,4,128]{3,1,0,2:T(1,128)S(1)}, u32[]{:S(2)}, u32[]{:S(2)}) async-start(s32[1,1,4,128]{3,1,0,2:T(1,128)} %bitcast.16), calls=%async_computation.2 | async-start | bytes 4096 | tf_op jit(solution)/shard_map/all_to_all | solution.py:34
  20.7 8.2 %all-to-all-done.2 = s32[1,1,4,128]{3,1,0,2:T(1,128)S(1)} async-done(((s32[1,1,4,128]{3,1,0,2:T(1,128)}), s32[1,1,4,128]{3,1,0,2:T(1,128)S(1)}, u32[]{:S(2)}, u32[]{:S(2)}) %all-to-all-start.2) | async-done | bytes 2080 | tf_op jit(solution)/shard_map/all_to_all | solution.py:34
  28.9 3.2 %all-to-all-start = ((f32[1,1,4,3,128]{4,3,1,0,2:T(4,128)}), f32[1,1,4,3,128]{4,3,1,0,2:T(4,128)S(1)}, u32[]{:S(2)}, u32[]{:S(2)}) async-start(f32[1,1,4,3,128]{4,3,1,0,2:T(4,128)} %copy.81), calls=%async_computation | async-start | bytes 16384 | tf_op jit(solution)/shard_map/all_to_all | solution.py:35
  32.7 1.3 fusion.35
  34.1 2.0 collective-permute-start.4
  37.3 7.6 %collective-permute-done.4 = f32[4,137,1]{2,1,0:T(8,128)S(1)} collective-permute-done((f32[4,137,1]{2,1,0:T(8,128)S(1)}, f32[4,137,1]{2,1,0:T(8,128)S(1)}, u32[]{:S(2)}, u32[]{:S(2)}) %collective-permute-start.4) | collective-permute-done | bytes 2224 | tf_op jit(solution)/shard_map/ppermute | solution.py:14
  44.9 3.5 %collective-permute-done.5 = f32[4,137,1]{2,1,0:T(8,128)} collective-permute-done((f32[4,137,1]{2,1,0:T(8,128)S(1)}, f32[4,137,1]{2,1,0:T(8,128)}, u32[]{:S(2)}, u32[]{:S(2)}) %collective-permute-start.5) | collective-permute-done | bytes 2224 | tf_op jit(solution)/shard_map/ppermute | solution.py:15
  48.4 1.3 fusion.31
  50.6 1.5 collective-permute-start.6
  52.1 1.5 collective-permute-start.7
  54.0 3.1 %gather_fusion.7 = f32[512]{0:T(512)S(1)} fusion(f32[70144]{0:T(1024)S(1)} %reshape.355, s32[1024]{0:T(1024)S(1)} %get-tuple-element.72), kind=kCustom, calls=%fused_computation.7 | custom fusion | bytes 6144 | tf_op jit(solution)/shard_map/gather | solution.py:61
  57.1 3.1 %gather_fusion.6 = f32[512]{0:T(512)S(1)} fusion(f32[70144]{0:T(1024)S(1)} %reshape.355, s32[1024]{0:T(1024)S(1)} %get-tuple-element.73), kind=kCustom, calls=%fused_computation.6 | custom fusion | bytes 6144 | tf_op jit(solution)/shard_map/gather | solution.py:61
  60.3 3.1 %gather_fusion.5 = f32[512]{0:T(512)S(1)} fusion(f32[70144]{0:T(1024)S(1)} %reshape.354, s32[1024]{0:T(1024)S(1)} %get-tuple-element.72), kind=kCustom, calls=%fused_computation.5 | custom fusion | bytes 6144 | tf_op jit(solution)/shard_map/gather | solution.py:61
  63.5 3.1 %gather_fusion.4 = f32[512]{0:T(512)S(1)} fusion(f32[70144]{0:T(1024)S(1)} %reshape.354, s32[1024]{0:T(1024)S(1)} %get-tuple-element.73), kind=kCustom, calls=%fused_computation.4 | custom fusion | bytes 6144 | tf_op jit(solution)/shard_map/gather | solution.py:61
  66.6 1.3 fusion.27
  68.7 2.4 %collective-permute-start.9 = (f32[4,137,1]{2,1,0:T(8,128)S(1)}, f32[4,137,1]{2,1,0:T(8,128)S(1)}, u32[]{:S(2)}, u32[]{:S(2)}) collective-permute-start(f32[4,137,1]{2,1,0:T(8,128)S(1)} %get-tuple-element.56), channel_id=1, source_target_pairs={{1,0},{2,1},{3,2},{0,3},{5,4},{6,5},{7,6},{4,7},{9,8},{10,9},{11,1... | collective-permute-start | bytes 6584 | tf_op jit(solution)/shard_map/ppermute | solution.py:15
  71.1 3.1 %gather_fusion.3 = f32[512]{0:T(512)S(1)} fusion(f32[70144]{0:T(1024)S(1)} %reshape.353, s32[1024]{0:T(1024)S(1)} %get-tuple-element.72), kind=kCustom, calls=%fused_computation.3 | custom fusion | bytes 6144 | tf_op jit(solution)/shard_map/gather | solution.py:61
  74.2 3.1 %gather_fusion.2 = f32[512]{0:T(512)S(1)} fusion(f32[70144]{0:T(1024)S(1)} %reshape.353, s32[1024]{0:T(1024)S(1)} %get-tuple-element.73), kind=kCustom, calls=%fused_computation.2 | custom fusion | bytes 6144 | tf_op jit(solution)/shard_map/gather | solution.py:61
  77.4 1.9 collective-permute-done.9
  79.7 3.1 %gather_fusion.1 = f32[512]{0:T(512)S(1)} fusion(f32[70144]{0:T(1024)S(1)} %reshape.352, s32[1024]{0:T(1024)S(1)} %get-tuple-element.72), kind=kCustom, calls=%fused_computation.1 | custom fusion | bytes 6144 | tf_op jit(solution)/shard_map/gather | solution.py:61
  82.8 3.1 %gather_fusion = f32[512]{0:T(512)S(1)} fusion(f32[70144]{0:T(1024)S(1)} %reshape.352, s32[1024]{0:T(1024)S(1)} %get-tuple-element.73), kind=kCustom, calls=%fused_computation | custom fusion | bytes 6144 | tf_op jit(solution)/shard_map/gather | solution.py:61
  86.0 1.3 collective-permute-start.10
  88.7 3.5 %scatter_custom_fusion = f32[280576]{0:T(1024)S(1)} fusion(s32[512]{0:T(512)S(1)} %fusion.42, f32[512]{0:T(512)S(1)} %get-tuple-element.67, f32[]{:T(128)} %constant.16.clone.1), kind=kCustom, calls=%fused_computation.10 | custom fusion | flops 512 | bytes 1122308 | tf_op jit(solution)/shard_map/scatter-add | solution.py:72
  92.2 3.7 %scatter_fusion = f32[280576]{0:T(1024)S(1)} fusion(f32[280576]{0:T(1024)S(1)} %scatter_custom_fusion, s32[512]{0:T(512)S(1)} %get-tuple-element.70, f32[512]{0:T(512)S(1)} %get-tuple-element.66), kind=kCustom, calls=%fused_computation.9 | custom fusion | flops 512 | bytes 8192 | tf_op jit(solution)/shard_map/scatter-add | solution.py:72
  96.8 1.3 collective-permute-start.11
  100.0 2.4 %collective-permute-done.11 = f32[4,137,128]{2,1,0:T(8,128)} collective-permute-done((f32[4,137,128]{2,1,0:T(8,128)}, f32[4,137,128]{2,1,0:T(8,128)}, u32[]{:S(2)}, u32[]{:S(2)}) %collective-permute-start.11) | collective-permute-done | bytes 280608 | tf_op jit(solution)/shard_map/ppermute | solution.py:23
  102.4 1.0 negate_add_fusion
  104.3 1.2 collective-permute-start.12
  108.4 3.0 %collective-permute-done.12 = f32[4,137,1]{2,1,0:T(8,128)} collective-permute-done((f32[4,137,1]{2,1,0:T(8,128)}, f32[4,137,1]{2,1,0:T(8,128)}, u32[]{:S(2)}, u32[]{:S(2)}) %collective-permute-start.12) | collective-permute-done | bytes 2224 | tf_op jit(solution)/shard_map/ppermute | solution.py:15
  111.4 6.2 %collective-permute-done.13 = f32[4,137,1]{2,1,0:T(8,128)} collective-permute-done((f32[4,137,1]{2,1,0:T(8,128)}, f32[4,137,1]{2,1,0:T(8,128)}, u32[]{:S(2)}, u32[]{:S(2)}) %collective-permute-start.13) | collective-permute-done | bytes 2224 | tf_op jit(solution)/shard_map/ppermute | solution.py:14
  117.6 1.4 fusion.19
  120.2 1.7 collective-permute-start.15
  122.2 4.7 %collective-permute-done.14 = f32[4,137,1]{2,1,0:T(8,128)S(1)} collective-permute-done((f32[4,137,1]{2,1,0:T(8,128)}, f32[4,137,1]{2,1,0:T(8,128)S(1)}, u32[]{:S(2)}, u32[]{:S(2)}) %collective-permute-start.14) | collective-permute-done | bytes 2224 | tf_op jit(solution)/shard_map/ppermute | solution.py:15
  126.9 6.5 %collective-permute-done.15 = f32[4,137,1]{2,1,0:T(8,128)} collective-permute-done((f32[4,137,1]{2,1,0:T(8,128)}, f32[4,137,1]{2,1,0:T(8,128)}, u32[]{:S(2)}, u32[]{:S(2)}) %collective-permute-start.15) | collective-permute-done | bytes 2224 | tf_op jit(solution)/shard_map/ppermute | solution.py:14
  133.4 1.3 fusion.14
  135.6 1.2 collective-permute-start.16
  137.9 5.8 %collective-permute-done.16 = f32[4,137,1]{2,1,0:T(8,128)S(1)} collective-permute-done((f32[4,137,1]{2,1,0:T(8,128)}, f32[4,137,1]{2,1,0:T(8,128)S(1)}, u32[]{:S(2)}, u32[]{:S(2)}) %collective-permute-start.16) | collective-permute-done | bytes 2224 | tf_op jit(solution)/shard_map/ppermute | solution.py:15
  143.7 7.2 %collective-permute-done.17 = f32[4,137,1]{2,1,0:T(8,128)S(1)} collective-permute-done((f32[4,137,1]{2,1,0:T(8,128)}, f32[4,137,1]{2,1,0:T(8,128)S(1)}, u32[]{:S(2)}, u32[]{:S(2)}) %collective-permute-start.17) | collective-permute-done | bytes 2224 | tf_op jit(solution)/shard_map/ppermute | solution.py:14
  151.7 1.7 collective-permute-start.19
  153.4 3.2 %all-to-all-start.3 = ((f32[1,1,4,128]{3,1,0,2:T(1,128)}), f32[1,1,4,128]{3,1,0,2:T(1,128)S(1)}, u32[]{:S(2)}, u32[]{:S(2)}) async-start(f32[1,1,4,128]{3,1,0,2:T(1,128)} %bitcast.58), calls=%async_computation.3 | async-start | bytes 4096 | tf_op jit(solution)/shard_map/all_to_all | solution.py:89
  156.9 10.0 %all-to-all-done.3 = f32[1,1,4,128]{3,1,0,2:T(1,128)S(1)} async-done(((f32[1,1,4,128]{3,1,0,2:T(1,128)}), f32[1,1,4,128]{3,1,0,2:T(1,128)S(1)}, u32[]{:S(2)}, u32[]{:S(2)}) %all-to-all-start.3) | async-done | bytes 2080 | tf_op jit(solution)/shard_map/all_to_all | solution.py:89
  169.2 48.6 %all-reduce = (f32[]{:T(128)}, f32[]{:T(128)}) all-reduce(f32[]{:T(128)S(6)} %mul.422, f32[]{:T(128)} %get-tuple-element.12), channel_id=1, replica_groups=mesh['tm'=8,'space'=4] {'tm','space'}, use_global_device_ids=true, to_apply=%region_2.3 | all-reduce | flops 2 | bytes 16 | tf_op jit(solution)/shard_map/psum | solution.py:87
  (109 shorter events, 23.0 us)
Async XLA Ops:
  1.9 14.3 %all-to-all-start.1 = ((s32[1,1,4]{1,0,2:T(1,128)}), s32[1,1,4]{1,0,2:T(1,128)S(1)}, u32[]{:S(2)}, u32[]{:S(2)}) async-start(s32[1,1,4]{1,0,2:T(1,128)} %copy.83), calls=%async_computation.1 | async-start | bytes 4096 | tf_op jit(solution)/shard_map/all_to_all | solution.py:36
  8.3 23.9 %collective-permute-start = (f32[4,137,1]{1,2,0:T(1,128)S(1)}, f32[4,137,1]{1,2,0:T(1,128)S(1)}, u32[]{:S(2)}, u32[]{:S(2)}) collective-permute-start(f32[4,137,1]{1,2,0:T(1,128)S(1)} %get-tuple-element.45), channel_id=1, source_target_pairs={{0,1},{1,2},{2,3},{3,0},{4,5},{5,6},{6,7},{7,4},{8,9},{9,10},{10,1... | collective-permute-start | bytes 6584 | tf_op jit(solution)/shard_map/ppermute | solution.py:14
  10.4 21.8 %collective-permute-start.1 = (f32[4,137,1]{1,2,0:T(1,128)S(1)}, f32[4,137,1]{1,2,0:T(1,128)S(1)}, u32[]{:S(2)}, u32[]{:S(2)}) collective-permute-start(f32[4,137,1]{1,2,0:T(1,128)S(1)} %get-tuple-element.46), channel_id=1, source_target_pairs={{1,0},{2,1},{3,2},{0,3},{5,4},{6,5},{7,6},{4,7},{9,8},{10,9},{11,1... | collective-permute-start | bytes 6584 | tf_op jit(solution)/shard_map/ppermute | solution.py:15
  13.2 6.3 %copy-start.10 = (f32[1,1,4,3,128]{4,2,3,1,0:T(4,128)S(1)}, f32[1,1,4,3,128]{4,2,3,1,0:T(4,128)}, u32[]{:S(2)}) copy-start(f32[1,1,4,3,128]{4,2,3,1,0:T(4,128)} %param.10) | copy-start | bytes 18436
  13.2 19.4 %collective-permute-start.2 = (f32[4,137,1]{2,1,0:T(8,128)}, f32[4,137,1]{2,1,0:T(8,128)S(1)}, u32[]{:S(2)}, u32[]{:S(2)}) collective-permute-start(f32[4,137,1]{2,1,0:T(8,128)} %get-tuple-element.61), channel_id=1, source_target_pairs={{0,1},{1,2},{2,3},{3,0},{4,5},{5,6},{6,7},{7,4},{8,9},{9,10},{10,1... | collective-permute-start | bytes 6584 | tf_op jit(solution)/shard_map/ppermute | solution.py:14
  14.3 18.4 %collective-permute-start.3 = (f32[4,137,1]{2,1,0:T(8,128)}, f32[4,137,1]{2,1,0:T(8,128)}, u32[]{:S(2)}, u32[]{:S(2)}) collective-permute-start(f32[4,137,1]{2,1,0:T(8,128)} %get-tuple-element.62), channel_id=1, source_target_pairs={{1,0},{2,1},{3,2},{0,3},{5,4},{6,5},{7,6},{4,7},{9,8},{10,9},{11,1... | collective-permute-start | bytes 6584 | tf_op jit(solution)/shard_map/ppermute | solution.py:15
  16.2 12.7 %all-to-all-start.2 = ((s32[1,1,4,128]{3,1,0,2:T(1,128)}), s32[1,1,4,128]{3,1,0,2:T(1,128)S(1)}, u32[]{:S(2)}, u32[]{:S(2)}) async-start(s32[1,1,4,128]{3,1,0,2:T(1,128)} %bitcast.16), calls=%async_computation.2 | async-start | bytes 4096 | tf_op jit(solution)/shard_map/all_to_all | solution.py:34
  20.2 59.1 %copy-start.4 = (f32[137,128]{1,0:T(8,128)}, f32[137,128]{1,0:T(8,128)S(1)}, u32[]{:S(2)}) copy-start(f32[137,128]{1,0:T(8,128)S(1)} %copy.69) | copy-start | bytes 210436
  20.5 46.1 %copy-start.2 = (f32[137,128]{1,0:T(8,128)}, f32[137,128]{1,0:T(8,128)S(1)}, u32[]{:S(2)}) copy-start(f32[137,128]{1,0:T(8,128)S(1)} %copy.70) | copy-start | bytes 210436
  28.9 42.1 %all-to-all-start = ((f32[1,1,4,3,128]{4,3,1,0,2:T(4,128)}), f32[1,1,4,3,128]{4,3,1,0,2:T(4,128)S(1)}, u32[]{:S(2)}, u32[]{:S(2)}) async-start(f32[1,1,4,3,128]{4,3,1,0,2:T(4,128)} %copy.81), calls=%async_computation | async-start | bytes 16384 | tf_op jit(solution)/shard_map/all_to_all | solution.py:35
  34.1 10.8 %collective-permute-start.4 = (f32[4,137,1]{2,1,0:T(8,128)S(1)}, f32[4,137,1]{2,1,0:T(8,128)S(1)}, u32[]{:S(2)}, u32[]{:S(2)}) collective-permute-start(f32[4,137,1]{2,1,0:T(8,128)S(1)} %get-tuple-element.59), channel_id=1, source_target_pairs={{0,1},{1,2},{2,3},{3,0},{4,5},{5,6},{6,7},{7,4},{8,9},{9,10},{10,1... | collective-permute-start | bytes 6584 | tf_op jit(solution)/shard_map/ppermute | solution.py:14
  36.1 12.3 %collective-permute-start.5 = (f32[4,137,1]{2,1,0:T(8,128)S(1)}, f32[4,137,1]{2,1,0:T(8,128)}, u32[]{:S(2)}, u32[]{:S(2)}) collective-permute-start(f32[4,137,1]{2,1,0:T(8,128)S(1)} %get-tuple-element.60), channel_id=1, source_target_pairs={{1,0},{2,1},{3,2},{0,3},{5,4},{6,5},{7,6},{4,7},{9,8},{10,9},{11,1... | collective-permute-start | bytes 6584 | tf_op jit(solution)/shard_map/ppermute | solution.py:15
  50.6 16.0 %collective-permute-start.6 = (f32[4,137,1]{2,1,0:T(8,128)}, f32[4,137,1]{2,1,0:T(8,128)S(1)}, u32[]{:S(2)}, u32[]{:S(2)}) collective-permute-start(f32[4,137,1]{2,1,0:T(8,128)} %get-tuple-element.57), channel_id=1, source_target_pairs={{0,1},{1,2},{2,3},{3,0},{4,5},{5,6},{6,7},{7,4},{8,9},{9,10},{10,1... | collective-permute-start | bytes 6584 | tf_op jit(solution)/shard_map/ppermute | solution.py:14
  52.1 14.5 %collective-permute-start.7 = (f32[4,137,1]{2,1,0:T(8,128)}, f32[4,137,1]{2,1,0:T(8,128)}, u32[]{:S(2)}, u32[]{:S(2)}) collective-permute-start(f32[4,137,1]{2,1,0:T(8,128)} %get-tuple-element.58), channel_id=1, source_target_pairs={{1,0},{2,1},{3,2},{0,3},{5,4},{6,5},{7,6},{4,7},{9,8},{10,9},{11,1... | collective-permute-start | bytes 6584 | tf_op jit(solution)/shard_map/ppermute | solution.py:15
  68.1 9.3 %collective-permute-start.8 = (f32[4,137,1]{2,1,0:T(8,128)S(1)}, f32[4,137,1]{2,1,0:T(8,128)S(1)}, u32[]{:S(2)}, u32[]{:S(2)}) collective-permute-start(f32[4,137,1]{2,1,0:T(8,128)S(1)} %get-tuple-element.55), channel_id=1, source_target_pairs={{0,1},{1,2},{2,3},{3,0},{4,5},{5,6},{6,7},{7,4},{8,9},{9,10},{10,1... | collective-permute-start | bytes 6584 | tf_op jit(solution)/shard_map/ppermute | solution.py:14
  68.7 10.7 %collective-permute-start.9 = (f32[4,137,1]{2,1,0:T(8,128)S(1)}, f32[4,137,1]{2,1,0:T(8,128)S(1)}, u32[]{:S(2)}, u32[]{:S(2)}) collective-permute-start(f32[4,137,1]{2,1,0:T(8,128)S(1)} %get-tuple-element.56), channel_id=1, source_target_pairs={{1,0},{2,1},{3,2},{0,3},{5,4},{6,5},{7,6},{4,7},{9,8},{10,9},{11,1... | collective-permute-start | bytes 6584 | tf_op jit(solution)/shard_map/ppermute | solution.py:15
  86.0 10.0 %collective-permute-start.10 = (f32[4,137,128]{2,1,0:T(8,128)S(1)}, f32[4,137,128]{2,1,0:T(8,128)S(1)}, u32[]{:S(2)}, u32[]{:S(2)}) collective-permute-start(f32[4,137,128]{2,1,0:T(8,128)S(1)} %fusion.23), channel_id=1, source_target_pairs={{0,4},{4,8},{8,12},{12,16},{16,20},{20,24},{24,28},{1,5},{5,9},{9,... | collective-permute-start | bytes 841736 | tf_op jit(solution)/shard_map/ppermute | solution.py:23
  92.2 3.7 %copy-start = (f32[1,4,137,128]{3,1,2,0:T(4,128)S(1)}, f32[1,4,137,128]{3,1,2,0:T(4,128)}, u32[]{:S(2)}) copy-start(f32[1,4,137,128]{3,1,2,0:T(4,128)} %param.6) | copy-start | bytes 841732
  92.2 3.7 %copy-start.9 = (f32[4,137]{1,0:T(4,128)S(1)}, f32[4,137]{1,0:T(4,128)}, u32[]{:S(2)}) copy-start(f32[4,137]{1,0:T(4,128)} %param.8) | copy-start | bytes 6580
  96.8 5.6 %collective-permute-start.11 = (f32[4,137,128]{2,1,0:T(8,128)}, f32[4,137,128]{2,1,0:T(8,128)}, u32[]{:S(2)}, u32[]{:S(2)}) collective-permute-start(f32[4,137,128]{2,1,0:T(8,128)} %broadcast_multiply_fusion), channel_id=1, source_target_pairs={{4,0},{8,4},{12,8},{16,12},{20,16},{24,20},{28,24},{5,1},{9,5},{13... | collective-permute-start | bytes 841736 | tf_op jit(solution)/shard_map/ppermute | solution.py:23
  104.3 7.0 %collective-permute-start.12 = (f32[4,137,1]{2,1,0:T(8,128)}, f32[4,137,1]{2,1,0:T(8,128)}, u32[]{:S(2)}, u32[]{:S(2)}) collective-permute-start(f32[4,137,1]{2,1,0:T(8,128)} %get-tuple-element.53), channel_id=1, source_target_pairs={{1,0},{2,1},{3,2},{0,3},{5,4},{6,5},{7,6},{4,7},{9,8},{10,9},{11,1... | collective-permute-start | bytes 6584 | tf_op jit(solution)/shard_map/ppermute | solution.py:15
  105.6 2.8 %copy-start.1 = (f32[70144]{0:T(1024)S(1)}, f32[70144]{0:T(1024)}, u32[]{:S(2)}) copy-start(f32[70144]{0:T(1024)} %get-tuple-element.21) | copy-start | bytes 841732
  105.6 12.0 %collective-permute-start.13 = (f32[4,137,1]{2,1,0:T(8,128)}, f32[4,137,1]{2,1,0:T(8,128)}, u32[]{:S(2)}, u32[]{:S(2)}) collective-permute-start(f32[4,137,1]{2,1,0:T(8,128)} %get-tuple-element.54), channel_id=1, source_target_pairs={{0,1},{1,2},{2,3},{3,0},{4,5},{5,6},{6,7},{7,4},{8,9},{9,10},{10,1... | collective-permute-start | bytes 6584 | tf_op jit(solution)/shard_map/ppermute | solution.py:14
  107.2 10.4 %copy-start.5 = (f32[137,128]{1,0:T(8,128)S(1)}, f32[137,128]{1,0:T(8,128)}, u32[]{:S(2)}) copy-start(f32[137,128]{1,0:T(8,128)} %copy-done.4) | copy-start | bytes 210436
  108.4 13.5 %copy-start.8 = (f32[137,130]{0,1:T(8,128)S(1)}, f32[137,130]{0,1:T(8,128)}, u32[]{:S(2)}) copy-start(f32[137,130]{0,1:T(8,128)} %get-tuple-element.29) | copy-start | bytes 213724
  119.0 3.1 %copy-start.7 = (f32[137,130]{0,1:T(8,128)S(1)}, f32[137,130]{0,1:T(8,128)}, u32[]{:S(2)}) copy-start(f32[137,130]{0,1:T(8,128)} %get-tuple-element.75) | copy-start | bytes 213724
  119.0 14.4 %copy-start.3 = (f32[137,128]{1,0:T(8,128)S(1)}, f32[137,128]{1,0:T(8,128)}, u32[]{:S(2)}) copy-start(f32[137,128]{1,0:T(8,128)} %copy-done.2) | copy-start | bytes 210436
  119.9 7.0 %collective-permute-start.14 = (f32[4,137,1]{2,1,0:T(8,128)}, f32[4,137,1]{2,1,0:T(8,128)S(1)}, u32[]{:S(2)}, u32[]{:S(2)}) collective-permute-start(f32[4,137,1]{2,1,0:T(8,128)} %get-tuple-element.51), channel_id=1, source_target_pairs={{1,0},{2,1},{3,2},{0,3},{5,4},{6,5},{7,6},{4,7},{9,8},{10,9},{11,1... | collective-permute-start | bytes 6584 | tf_op jit(solution)/shard_map/ppermute | solution.py:15
  120.2 13.2 %collective-permute-start.15 = (f32[4,137,1]{2,1,0:T(8,128)}, f32[4,137,1]{2,1,0:T(8,128)}, u32[]{:S(2)}, u32[]{:S(2)}) collective-permute-start(f32[4,137,1]{2,1,0:T(8,128)} %get-tuple-element.52), channel_id=1, source_target_pairs={{0,1},{1,2},{2,3},{3,0},{4,5},{5,6},{6,7},{7,4},{8,9},{9,10},{10,1... | collective-permute-start | bytes 6584 | tf_op jit(solution)/shard_map/ppermute | solution.py:14
  122.2 15.4 %copy-start.6 = (f32[137,130]{0,1:T(8,128)S(1)}, f32[137,130]{0,1:T(8,128)}, u32[]{:S(2)}) copy-start(f32[137,130]{0,1:T(8,128)} %get-tuple-element.28) | copy-start | bytes 213724
  135.6 8.1 %collective-permute-start.16 = (f32[4,137,1]{2,1,0:T(8,128)}, f32[4,137,1]{2,1,0:T(8,128)S(1)}, u32[]{:S(2)}, u32[]{:S(2)}) collective-permute-start(f32[4,137,1]{2,1,0:T(8,128)} %get-tuple-element.49), channel_id=1, source_target_pairs={{1,0},{2,1},{3,2},{0,3},{5,4},{6,5},{7,6},{4,7},{9,8},{10,9},{11,1... | collective-permute-start | bytes 6584 | tf_op jit(solution)/shard_map/ppermute | solution.py:15
  136.8 14.1 %collective-permute-start.17 = (f32[4,137,1]{2,1,0:T(8,128)}, f32[4,137,1]{2,1,0:T(8,128)S(1)}, u32[]{:S(2)}, u32[]{:S(2)}) collective-permute-start(f32[4,137,1]{2,1,0:T(8,128)} %get-tuple-element.50), channel_id=1, source_target_pairs={{0,1},{1,2},{2,3},{3,0},{4,5},{5,6},{6,7},{7,4},{8,9},{9,10},{10,1... | collective-permute-start | bytes 6584 | tf_op jit(solution)/shard_map/ppermute | solution.py:14
  151.4 15.6 %collective-permute-start.18 = (f32[4,137,1]{2,1,0:T(8,128)S(1)}, f32[4,137,1]{2,1,0:T(8,128)S(1)}, u32[]{:S(2)}, u32[]{:S(2)}) collective-permute-start(f32[4,137,1]{2,1,0:T(8,128)S(1)} %get-tuple-element.47), channel_id=1, source_target_pairs={{1,0},{2,1},{3,2},{0,3},{5,4},{6,5},{7,6},{4,7},{9,8},{10,9},{11,1... | collective-permute-start | bytes 6584 | tf_op jit(solution)/shard_map/ppermute | solution.py:15
  151.7 15.2 %collective-permute-start.19 = (f32[4,137,1]{2,1,0:T(8,128)S(1)}, f32[4,137,1]{2,1,0:T(8,128)S(1)}, u32[]{:S(2)}, u32[]{:S(2)}) collective-permute-start(f32[4,137,1]{2,1,0:T(8,128)S(1)} %get-tuple-element.48), channel_id=1, source_target_pairs={{0,1},{1,2},{2,3},{3,0},{4,5},{5,6},{6,7},{7,4},{8,9},{9,10},{10,1... | collective-permute-start | bytes 6584 | tf_op jit(solution)/shard_map/ppermute | solution.py:14
  153.4 13.5 %all-to-all-start.3 = ((f32[1,1,4,128]{3,1,0,2:T(1,128)}), f32[1,1,4,128]{3,1,0,2:T(1,128)S(1)}, u32[]{:S(2)}, u32[]{:S(2)}) async-start(f32[1,1,4,128]{3,1,0,2:T(1,128)} %bitcast.58), calls=%async_computation.3 | async-start | bytes 4096 | tf_op jit(solution)/shard_map/all_to_all | solution.py:89
where the time goes:
time: 221 us
  waiting for transfers between devices  67.2 us (30%)
  blocking collectives  48.6 us (22%)
  local copies, waits for them, and re-layouts  41.5 us (19%)
  starting transfers between devices  40.5 us (18%)
  other arithmetic  18.9 us (9%)
  between operations  4 us (2%)
    psum x1, blocking collectives, on_device(): cost, norm = lax.psum((cost_part, norm_part), ('tm', 'space'))  48.6 us
    ppermute x9, waiting for transfers between devices, padded_2(): before = lax.ppermute(last, axis, up)  27.5 us
    gather x8, local copies, waits for them, and re-layouts, on_device(): seen = weight * line[flat] + (1.0 - weight) * line[flat + 1]  25.1 us
    ppermute x9, waiting for transfers between devices, padded_2(): after = lax.ppermute(initial, axis, down)  19 us
    ppermute x9, starting transfers between devices, padded_2(): before = lax.ppermute(last, axis, up)  12.2 us
    ppermute x9, starting transfers between devices, padded_2(): after = lax.ppermute(initial, axis, down)  10.8 us
    all_to_all x1, waiting for transfers between devices, on_device(): lax.all_to_all(departed[None, None], 'space', split_axis=2, concat_axis=2...  10 us
    all_to_all x1, waiting for transfers between devices, on_device(): lax.all_to_all(obs_code, 'space', split_axis=2, concat_axis=2, tiled=True)  8.22 us
  transfers between devices with their start and end apart: 24, of which 12 were waited for; matrix products, arithmetic and copies ran while one was open for 19% of the time, Pallas kernels for 0%

commit v1 on v0

v1 whole, which is shorter than its diff:
```python
import functools
import jax
import jax.numpy as jnp
from jax import lax
from jax.experimental import pallas as pl
from jax.experimental.pallas import tpu as pltpu
from jax.sharding import PartitionSpec as P

MESH = pl.DeviceIdType.MESH
LANES = 128
GATHER_PARTS = 3
SCATTER_PARTS = 2


def split(value, parts):
    out = []
    for part in range(parts):
        piece = value.astype(jnp.bfloat16)
        out.append(piece)
        if part + 1 < parts:
            value = value - piece.astype(jnp.float32)
    return out


def kernel(
    nt, ns, nf, lev, steps, inc_ref, cour_ref, ew_ref, code_ref, val_ref, cnt_ref,
    out_ref, dep_ref,
    xc, rem, ew_pad, edges, obs_out, obs_in, onehot, weights, parts, pieces, forcing,
    end, prev, nxt, grad, spill, spill_in, dep_out, dep_in, sums, sums_in, totals, totals_in,
    edge_s, edge_r, obs_s, obs_r, nxt_s, nxt_r, prev_s, prev_r, spill_s, spill_r,
    dep_s, dep_r, sum_s, sum_r, tot_s, tot_r,
):
    cd = LANES
    tiles = nf + 1
    wide = tiles * LANES
    gap = LANES // nf
    extra = lev - LANES
    per_state = nf * lev * cd
    slots = ns * LANES
    ring = cd + 8
    k = lax.axis_index("tm")
    me = lax.axis_index("space")
    f32 = jnp.float32

    def space_peer(i):
        return lax.rem(me + i, ns)

    def tm_peer(i):
        return lax.rem(k + i, nt)

    barrier = pltpu.get_barrier_semaphore()
    for i in range(1, ns):
        pl.semaphore_signal(barrier, inc=1, device_id=(k, space_peer(i)), device_id_type=MESH)
    for i in range(1, nt):
        pl.semaphore_signal(barrier, inc=1, device_id=(tm_peer(i), me), device_id_type=MESH)

    rem[...] = jnp.zeros_like(rem)
    for f in range(nf):
        rem[0, f * gap : f * gap + extra, :] = inc_ref[0, f, LANES:lev, :]
        for n in range(steps):
            rem[1 + n, f * gap : f * gap + extra, :] = cour_ref[0, n, LANES:lev, :]
    for f in range(nf):
        xc[f, 0:cd, :] = inc_ref[0, f, 0:LANES, :].T
    xc[nf, 0:cd, :] = rem[0].T
    for n in range(steps):
        xc[tiles + n, 0:cd, :] = cour_ref[0, n, 0:LANES, :].T
        xc[tiles + steps + n, 0:cd, :] = rem[1 + n].T
    lane_row = lax.broadcasted_iota(jnp.int32, (1, LANES), 1)
    for d in range(ns):
        used = lane_row < cnt_ref[0, 0, d]
        obs_out[d, 0:1, :] = jnp.where(used, code_ref[0, 0, d : d + 1, :], -1).astype(f32)
        obs_out[d, 1:4, :] = val_ref[0, 0, d]

    pl.semaphore_wait(barrier, ns - 1 + nt - 1)

    def remote(src, dst, send, recv, target):
        return pltpu.make_async_remote_copy(
            src_ref=src, dst_ref=dst, send_sem=send, recv_sem=recv,
            device_id=target, device_id_type=MESH,
        )

    left, right = space_peer(ns - 1), space_peer(1)
    edge_copies = [
        remote(xc.at[:, 0:8, :], edges.at[0], edge_s.at[0], edge_r.at[0], (k, left)),
        remote(xc.at[:, cd - 8 : cd, :], edges.at[1], edge_s.at[1], edge_r.at[1], (k, right)),
    ]
    obs_copies = [
        remote(
            obs_out.at[space_peer(i)], obs_in.at[me], obs_s.at[i], obs_r.at[i], (k, space_peer(i))
        )
        for i in range(1, ns)
    ]
    for copy in obs_copies + edge_copies:
        copy.start()
    not_first, not_last = k > 0, k < nt - 1
    before, after = lax.max(k - 1, 0), lax.min(k + 1, nt - 1)
    nxt_copy = remote(
        xc.at[0:tiles, 0:cd, :], nxt, nxt_s.at[0], nxt_r.at[0], (before, me)
    )

    @pl.when(not_first)
    def _():
        nxt_copy.start()

    @pl.when(jnp.logical_not(not_last))
    def _():
        nxt[...] = jnp.zeros_like(nxt)

    @pl.when(jnp.logical_not(not_first))
    def _():
        prev[...] = jnp.zeros_like(prev)

    obs_in[me] = obs_out[me]
    ew_pad[...] = jnp.zeros_like(ew_pad)
    for f in range(nf):
        ew_pad[f : f + 1, 0:extra] = ew_ref[f : f + 1, LANES:lev]
    ew_rows = [ew_ref[f : f + 1, 0:LANES] for f in range(nf)]
    ew_last = ew_pad[0:1, :]
    for f in range(1, nf):
        ew_last = ew_last + pltpu.roll(ew_pad[f : f + 1, :], f * gap, 1)
    ew_rows.append(ew_last)

    for copy in obs_copies:
        copy.wait_recv()

    def gathered(row):
        return jnp.concatenate([obs_in[s, row : row + 1, :] for s in range(ns)], axis=1)

    code = gathered(0).astype(jnp.int32)
    innovation, weight, rinv = gathered(1), gathered(2), gathered(3)
    when = jnp.zeros_like(code)
    for n in range(1, steps):
        when = when + (code >= n * per_state).astype(jnp.int32)
    flat = code - when * per_state
    row = lax.shift_right_arithmetic(flat, 7)
    column = jnp.bitwise_and(flat, LANES - 1)
    field = jnp.zeros_like(code)
    for f in range(1, nf):
        field = field + (row >= f * lev).astype(jnp.int32)
    level = row - field * lev
    place = jnp.where(
        level < LANES, field * LANES + level, nf * LANES + field * gap + level - LANES
    )
    key = when * wide + place
    line = lax.broadcasted_iota(jnp.int32, (LANES, LANES), 0)
    for s in range(ns):
        block = slice(s * LANES, (s + 1) * LANES)
        key_s = key[:, block]
        for t in range(steps * tiles):
            hit = line == key_s - t * LANES
            onehot[t * LANES : (t + 1) * LANES, block] = jnp.where(hit, 1.0, 0.0).astype(
                jnp.bfloat16
            )
        col_s, w_s = column[:, block], weight[:, block]
        weights[:, block] = jnp.where(line == col_s, w_s, 0.0) + jnp.where(
            line == col_s + 1, 1.0 - w_s, 0.0
        )

    for copy in edge_copies:
        copy.wait_recv()
    sub = lax.broadcasted_iota(jnp.int32, (8, LANES), 0)
    for t in range(tiles + 2 * steps):
        xc[t, cd:ring, :] = jnp.where(sub < 4, edges[0, t], edges[1, t])

    def courant_of(t, n):
        return xc[tiles + n if t < nf else tiles + steps + n]

    prev_copies = []
    for t in range(tiles):
        x = xc[t]
        for n in range(steps):
            c = courant_of(t, n)
            lower = pltpu.roll(x, 1, 0)
            upper = pltpu.roll(x, ring - 1, 0)
            x = x + (0.5 * c) * ((lower - upper) + c * ((lower + upper) - 2.0 * x))
            at = (n * tiles + t) * LANES
            for p, piece in enumerate(split(x[0:cd], GATHER_PARTS)):
                parts[p * cd : (p + 1) * cd, at : at + LANES] = piece
        end[t] = x[0:cd]
        copy = remote(end.at[t], prev.at[t], prev_s.at[t], prev_r.at[t], (after, me))
        prev_copies.append(copy)
        pl.when(not_last)(copy.start)

    seen_parts = jnp.dot(parts[...], onehot[...], preferred_element_type=f32)
    seen = seen_parts[0:cd]
    for p in range(1, GATHER_PARTS):
        seen = seen + seen_parts[p * cd : (p + 1) * cd]
    hx = jnp.sum(seen * weights[...], axis=0, keepdims=True)
    departed = jnp.where(code >= 0, hx - innovation, 0.0)
    pushed = rinv * departed
    for s in range(ns):
        dep_out[s, 0:1, :] = departed[:, s * LANES : (s + 1) * LANES]
    dep_copies = [
        remote(
            dep_out.at[space_peer(i)], dep_in.at[me], dep_s.at[i], dep_r.at[i], (k, space_peer(i))
        )
        for i in range(1, ns)
    ]
    for copy in dep_copies:
        copy.start()
    dep_in[me] = dep_out[me]
    for p, piece in enumerate(split(weights[...] * pushed, SCATTER_PARTS)):
        pieces[p * cd : (p + 1) * cd, :] = piece
    for n in range(steps):
        part = lax.dot_general(
            pieces[...],
            onehot[n * wide : (n + 1) * wide, :],
            (((1,), (1,)), ((), ())),
            preferred_element_type=f32,
        )
        total = part[0:cd]
        for p in range(1, SCATTER_PARTS):
            total = total + part[p * cd : (p + 1) * cd]
        forcing[n] = total

    pl.when(not_last)(nxt_copy.wait_recv)
    share = jnp.where(not_last, 1.0, 0.0)
    for t in range(tiles):
        lanes = slice(t * LANES, (t + 1) * LANES)
        own = forcing[steps - 1, :, lanes] - (share * ew_rows[t]) * (nxt[t] - end[t])
        lam = jnp.concatenate([own, jnp.zeros((8, LANES), f32)], axis=0)
        for n in reversed(range(steps)):
            c = courant_of(t, n)
            u = (0.5 * c) * lam
            v = c * u
            lam = (lam - 2.0 * v) + (pltpu.roll(u + v, ring - 1, 0) + pltpu.roll(v - u, 1, 0))
            if n > 0:
                lam = jnp.concatenate(
                    [lam[0:cd] + forcing[n - 1, :, lanes], lam[cd:ring]], axis=0
                )
        grad[t] = lam[0:cd]
        spill[t] = lam[cd:ring]
    spill_copies = [
        remote(spill, spill_in.at[0], spill_s.at[0], spill_r.at[0], (k, left)),
        remote(spill, spill_in.at[1], spill_s.at[1], spill_r.at[1], (k, right)),
    ]
    for copy in spill_copies:
        copy.start()

    def folded(value):
        return jnp.sum(value.reshape(-1, 8, LANES), axis=0)

    cost = jnp.zeros((8, LANES), f32)
    norm = jnp.zeros((8, LANES), f32)
    for t in range(tiles):
        pl.when(not_first)(prev_copies[t].wait_recv)
        jump = xc[t, 0:cd, :] - prev[t]
        weighted = ew_rows[t] * jump
        cost = cost + folded(weighted * jump)
        g = grad[t] + weighted
        grad[t] = g
        inner = g[8 : cd - 8]
        norm = norm + folded(inner * inner)
    obs_cost = jnp.zeros((1, LANES), f32)
    for s in range(ns):
        block = slice(s * LANES, (s + 1) * LANES)
        obs_cost = obs_cost + pushed[:, block] * departed[:, block]
    sums[0] = cost + jnp.where(sub == 0, obs_cost, 0.0)
    for copy in spill_copies:
        copy.wait_recv()
    for t in range(tiles):
        low = grad[t, 0:8, :] + jnp.where(sub < 4, spill_in[1, t], 0.0)
        high = grad[t, cd - 8 : cd, :] + jnp.where(sub < 4, 0.0, spill_in[0, t])
        grad[t, 0:8, :] = low
        grad[t, cd - 8 : cd, :] = high
        norm = norm + (low * low + high * high)
    sums[1] = norm

    sum_copies = [
        remote(sums, sums_in.at[i], sum_s.at[i], sum_r.at[i], (k, space_peer(i)))
        for i in range(1, ns)
    ]
    for copy in sum_copies:
        copy.start()
    for t in range(tiles):
        grad[t] = grad[t].T
    for copy in sum_copies:
        copy.wait_recv()
    total = sums[...]
    for i in range(1, ns):
        total = total + sums_in[i]
    totals[...] = total
    total_copies = [
        remote(totals, totals_in.at[i], tot_s.at[i], tot_r.at[i], (tm_peer(i), me))
        for i in range(1, nt)
    ]
    for copy in total_copies:
        copy.start()
    for copy in dep_copies:
        copy.wait_recv()
    for d in range(ns):
        dep_ref[0, 0, d : d + 1, :] = dep_in[d, 0:1, :]
    for copy in edge_copies + obs_copies + dep_copies + spill_copies + sum_copies:
        copy.wait_send()
    pl.when(not_first)(nxt_copy.wait_send)
    for copy in prev_copies:
        pl.when(not_last)(copy.wait_send)
    for copy in total_copies:
        copy.wait_recv()
    total = totals[...]
    for i in range(1, nt):
        total = total + totals_in[i]
    flat_total = jnp.sum(jnp.sum(total, axis=1, keepdims=True), axis=2, keepdims=True)
    ratio = 0.5 * flat_total[0] / flat_total[1]
    for f in range(nf):
        out_ref[0, f, 0:LANES, :] = inc_ref[0, f, 0:LANES, :] - ratio * grad[f]
        out_ref[0, f, LANES:lev, :] = (
            inc_ref[0, f, LANES:lev, :] - ratio * grad[nf, f * gap : f * gap + extra, :]
        )
    for copy in total_copies:
        copy.wait_send()


def solution(mesh):
    nt, ns = mesh.shape["tm"], mesh.shape["space"]
    in_specs = (
        P("tm", None, None, "space"),
        P("tm", None, None, "space"),
        P(),
        P("tm", "space", None, None),
        P("tm", "space", None, None, None),
        P("tm", "space", None),
    )
    out_specs = (P("tm", None, None, "space"), P("tm", "space", None, None))

    def on_device(increment, courant, error_weight, obs_code, obs_values, obs_count):
        _, nf, lev, cd = increment.shape
        steps = courant.shape[1]
        tiles = nf + 1
        wide = tiles * LANES
        slots = ns * LANES
        f32, bf16 = jnp.float32, jnp.bfloat16
        vmem = pl.BlockSpec(memory_space=pltpu.VMEM)
        dma = pltpu.SemaphoreType.DMA
        state = pltpu.VMEM((tiles, cd, LANES), f32)
        return pl.pallas_call(
            functools.partial(kernel, nt, ns, nf, lev, steps),
            out_shape=(
                jax.ShapeDtypeStruct(increment.shape, f32),
                jax.ShapeDtypeStruct(obs_code.shape, f32),
            ),
            in_specs=[vmem] * 5 + [pl.BlockSpec(memory_space=pltpu.SMEM)],
            out_specs=(vmem, vmem),
            scratch_shapes=[
                pltpu.VMEM((tiles + 2 * steps, cd + 8, LANES), f32),
                pltpu.VMEM((1 + steps, LANES, LANES), f32),
                pltpu.VMEM((8, LANES), f32),
                pltpu.VMEM((2, tiles + 2 * steps, 8, LANES), f32),
                pltpu.VMEM((ns, 8, LANES), f32),
                pltpu.VMEM((ns, 8, LANES), f32),
                pltpu.VMEM((steps * wide, slots), bf16),
                pltpu.VMEM((cd, slots), f32),
                pltpu.VMEM((GATHER_PARTS * cd, steps * wide), bf16),
                pltpu.VMEM((SCATTER_PARTS * cd, slots), bf16),
                pltpu.VMEM((steps, cd, wide), f32),
                state,
                state,
                state,
                state,
                pltpu.VMEM((tiles, 8, LANES), f32),
                pltpu.VMEM((2, tiles, 8, LANES), f32),
                pltpu.VMEM((ns, 8, LANES), f32),
                pltpu.VMEM((ns, 8, LANES), f32),
                pltpu.VMEM((2, 8, LANES), f32),
                pltpu.VMEM((ns, 2, 8, LANES), f32),
                pltpu.VMEM((2, 8, LANES), f32),
                pltpu.VMEM((nt, 2, 8, LANES), f32),
                dma((2,)), dma((2,)),
                dma((ns,)), dma((ns,)),
                dma((1,)), dma((1,)),
                dma((tiles,)), dma((tiles,)),
                dma((2,)), dma((2,)),
                dma((ns,)), dma((ns,)),
                dma((ns,)), dma((ns,)),
                dma((nt,)), dma((nt,)),
            ],
            compiler_params=pltpu.CompilerParams(
                collective_id=0, has_side_effects=True, vmem_limit_bytes=40 * 1024 * 1024
            ),
        )(increment, courant, error_weight, obs_code, obs_values, obs_count)

    return jax.shard_map(
        on_device, mesh=mesh, in_specs=in_specs, out_specs=out_specs, check_vma=False
    )
```

time: 221 us -> 29.8 us (0.13)
  waiting for transfers between devices: 67.2 us -> 0 us
  blocking collectives: 48.6 us -> 0 us
  starting transfers between devices: 40.5 us -> 0 us
  local copies, waits for them, and re-layouts: 41.5 us -> 3.8 us
  Pallas kernels: 0 us -> 25 us
  other arithmetic: 18.9 us -> 0 us
  between operations: 4 us -> 0.67 us
    ppermute x20 -> x0, waiting for transfers between devices: 48.9 us -> none  [the longest x9 27.5 us: padded_2(): before = lax.ppermute(last, axis, up)]
    psum x1 -> x0, blocking collectives: 48.6 us -> none  [on_device(): cost, norm = lax.psum((cost_part, norm_part), ('tm', 'space'))]
    ppermute x20 -> x0, starting transfers between devices: 25.6 us -> none  [the longest x9 12.2 us: padded_2(): before = lax.ppermute(last, axis, up)]
    gather x8 -> x0, local copies, waits for them, and re-layouts: 25.1 us -> none  [on_device(): seen = weight * line[flat] + (1.0 - weight) * line[flat + 1]]
    pallas_call x0 -> x1, Pallas kernels: none -> 25 us  [on_device(): pl.pallas_call(functools.partial(kernel, nt, ns, nf, lev, steps), out_sha...]
    all_to_all x4 -> x0, waiting for transfers between devices: 18.2 us -> none  [the longest x1 10 us: on_device(): lax.all_to_all(departed[None, None], 'space', split_axis=2, concat_axis=2...]
    all_to_all x4 -> x0, starting transfers between devices: 14.9 us -> none  [the longest x1 5.16 us: on_device(): lax.all_to_all(obs_count, 'space', split_axis=2, concat_axis=2, tiled=True)]
    slice x31 -> x0, local copies, waits for them, and re-layouts: 8.71 us -> none  [the longest x4 2.91 us: padded_2(): initial = lax.slice_in_dim(array, 0, width, axis=dim)]
  transfers between devices with their start and end apart: 24 -> 0, of which waited for: 12 -> 0; matrix products, arithmetic and copies ran while one was open for 19% -> 0% of each run, Pallas kernels for 0% -> 0%
where the time goes in v1:
time: 29.8 us; the launch traced here: 29.5 us
  Pallas kernels  25 us (84%)
  local copies, waits for them, and re-layouts  3.8 us (13%)
  between operations  0.67 us (2%)
    pallas_call x1, Pallas kernels, on_device(): pl.pallas_call(functools.partial(kernel, nt, ns, nf, lev, steps), out_sha...  25 us
    unnamed x12, local copies, waits for them, and re-layouts  2.98 us
    pallas_call x1, local copies, waits for them, and re-layouts, on_device(): pl.pallas_call(functools.partial(kernel, nt, ns, nf, lev, steps), out_sha...  0.82 us

profile of v1, /device:TPU:0, one launch (start us, length us, event | category | flops | bytes accessed | tf_op | source)
XLA Modules:
  0.0 29.5 jit_solution(6616744021044441895)
XLA Ops:
  0.6 0.7 %copy.10.val_ref = f32[1,1,4,3,128]{4,3,2,1,0:T(4,128)S(1)} copy(f32[1,1,4,3,128]{4,2,3,1,0:T(4,128)} %param.10) | data formatting | bytes 12288 | tf_op args[4]
  1.3 0.0 copy-start.3
  1.3 1.0 %copy.8.inc_ref = f32[1,4,137,128]{3,2,1,0:T(8,128)S(1)} copy(f32[1,4,137,128]{3,1,2,0:T(4,128)} %param.6) | data formatting | bytes 561152 | tf_op args[0]
  2.4 0.0 copy-done.3
  2.4 0.0 copy-start
  2.4 0.0 copy-start.1
  2.4 0.0 copy-start.2
  2.4 0.6 %copy-done = f32[4,137]{1,0:T(4,128)S(1)} copy-done((f32[4,137]{1,0:T(4,128)S(1)}, f32[4,137]{1,0:T(4,128)}, u32[]{:S(2)}) %copy-start) | copy-done | bytes 2216
  3.1 0.0 copy-done.1
  3.1 0.0 copy-done.2
  3.1 25.0 %shard_map.77 = (f32[1,4,137,128]{3,2,1,0:T(8,128)S(1)}, f32[1,1,4,128]{3,2,1,0:T(4,128)S(1)}) custom-call(f32[1,4,137,128]{3,2,1,0:T(8,128)S(1)} %copy.8.inc_ref, f32[1,4,137,128]{3,2,1,0:T(8,128)S(1)} %copy.9.cour_ref, f32[4,137]{1,0:T(4,128)S(1)} %copy-done, s32[1,1,4,128]{3,2,1,0:T(4,128)S(1)} %copy-done.1, f32[1,1,4,3,128]{4,3,2,1,0:T(4,128)S(1)} %copy.10.val_ref, ...), custom_call_target="tpu_custom_call" | custom-call | tf_op jit(solution)/shard_map/pallas_call | solution.py:336
  28.1 0.8 %copy.11 = f32[1,4,137,128]{3,1,2,0:T(4,128)} copy(f32[1,4,137,128]{3,2,1,0:T(8,128)S(1)} %get-tuple-element.2) | data formatting | bytes 561152 | tf_op jit(solution)/shard_map/pallas_call | solution.py:336
  28.9 0.6 %copy.13 = f32[1,1,4,128]{3,2,1,0:T(4,128)} copy(f32[1,1,4,128]{3,2,1,0:T(4,128)S(1)} %get-tuple-element.7) | data formatting | bytes 4096
  (1 shorter events, 0.0 us)
Async XLA Ops:
  1.3 1.0 %copy-start.3 = (f32[1,4,137,128]{3,1,2,0:T(4,128)S(1)}, f32[1,4,137,128]{3,1,2,0:T(4,128)}, u32[]{:S(2)}) copy-start(f32[1,4,137,128]{3,1,2,0:T(4,128)} %param.7) | copy-start | bytes 841732
  2.4 0.7 %copy-start = (f32[4,137]{1,0:T(4,128)S(1)}, f32[4,137]{1,0:T(4,128)}, u32[]{:S(2)}) copy-start(f32[4,137]{1,0:T(4,128)} %ew_ref.1) | copy-start | bytes 6580
  2.4 0.7 %copy-start.1 = (s32[1,1,4,128]{3,2,1,0:T(4,128)S(1)}, s32[1,1,4,128]{3,2,1,0:T(4,128)}, u32[]{:S(2)}) copy-start(s32[1,1,4,128]{3,2,1,0:T(4,128)} %code_ref.1) | copy-start | bytes 6148
  2.4 0.7 %copy-start.2 = (s32[1,1,4]{2,1,0:T(1,128)S(1)}, s32[1,1,4]{2,1,0:T(1,128)}, u32[]{:S(2)}) copy-start(s32[1,1,4]{2,1,0:T(1,128)} %cnt_ref.1) | copy-start | bytes 52
